TPU v7x, 512 devices: a whole 4x4x16 slice. The times are simulated.
512 devices in a mesh: dx: 16 (over z_lo, core), dy: 8 (over z_hi, x), tp: 4 (over y).
Axes of the slice: x: 4, y: 4, z: 16 (z_hi: 2, z_lo: 8; z = z_hi * 8 + z_lo), core: 2. Of those that a mesh axis runs over, the one named last changes fastest.
Arguments:
- normed: bfloat16 [16384, 4096], P(('dx', 'dy'), 'tp'), may hold values from -6 to 6
- key_weight: bfloat16 [4096, 512], P(None, 'tp'), may hold values from -0.09375 to 0.09375
- key_grad: bfloat16 [16384, 512], P(('dx', 'dy'), 'tp'), may hold values from -6 to 6
Outputs:
- input_grad: bfloat16 [16384, 4096], P(('dx', 'dy'), 'tp')
- weight_grad: bfloat16 [4096, 512], P(None, 'tp')
- bias_grad: float32 [512], P('tp')
All inputs are finite; a program needn't handle non-finite values.
Results may differ from a plain program's by a relative error of at most 0.015.
Values may be sent and summed in bfloat16 or wider, within the bound.
A program may use at most 64 MiB of HBM per device.

v0:
```python
import math

import jax
import jax.numpy as jnp
from jax import lax
from jax.sharding import PartitionSpec as P

HD = 128
SEQ = 4096


def rope_back(grad, first_row):
    row_count = grad.shape[0]
    values = grad.astype(jnp.float32).reshape(row_count, -1, HD)
    half_size = HD // 2
    positions = ((first_row + jnp.arange(row_count, dtype=jnp.int32)) % SEQ).astype(jnp.float32)
    inverse_rates = jnp.exp(
        jnp.arange(half_size, dtype=jnp.float32) * (-2.0 * math.log(1000000.0) / HD)
    )
    angles = positions[:, None] * inverse_rates[None, :]
    cosine = jnp.cos(angles)[:, None, :]
    sines = jnp.sin(angles)[:, None, :]
    first_half = values[:, :, :half_size]
    second_half = values[:, :, half_size:]
    result = jnp.concatenate(
        [first_half * cosine + second_half * sines, second_half * cosine - first_half * sines],
        axis=2,
    )
    return result.reshape(row_count, -1)


def body(normed, key_weight, key_grad):
    row_count = normed.shape[0]
    replicas = lax.axis_size("dx") * lax.axis_size("dy")
    shard_number = lax.axis_index("dx") * lax.axis_size("dy") + lax.axis_index("dy")
    raw_grad = rope_back(key_grad, shard_number * row_count).astype(jnp.bfloat16)
    local_weight = (
        jnp.einsum(
            "tk,th->kh",
            lax.all_gather(normed, "tp", axis=1, tiled=True),
            raw_grad,
            preferred_element_type=jnp.float32,
        )
        / replicas
    )
    local_bias = jnp.sum(raw_grad.astype(jnp.float32), axis=0) / replicas
    partial_terms = jnp.einsum(
        "th,dh->td", raw_grad, key_weight, preferred_element_type=jnp.float32
    )
    input_grad = lax.psum_scatter(
        partial_terms.astype(jnp.bfloat16), "tp", scatter_dimension=1, tiled=True
    )
    weight_total, bias_total = lax.psum((local_weight, local_bias), ("dx", "dy"))
    weight_grad = weight_total.astype(jnp.bfloat16)
    return (input_grad, weight_grad, bias_total)


def solution(mesh):
    placed = (P(("dx", "dy"), "tp"), P(None, "tp"), P(("dx", "dy"), "tp"))
    return jax.shard_map(
        body,
        mesh=mesh,
        in_specs=placed,
        out_specs=(P(("dx", "dy"), "tp"), P(None, "tp"), P("tp")),
        check_vma=False,
    )
```

profile of v0, /device:TPU:1, one launch (start us, length us, event | category | flops | bytes accessed | tf_op | source)
XLA Modules:
  0.0 1102.5 jit_solution(10500713955856085927)
XLA Ops:
  7.2 0.0 copy-start
  7.2 0.0 all-gather.2.cloned.1.call-start
  7.2 0.7 all-gather.2.cloned.1.call-update
  7.9 0.0 reduce-scatter.2.cloned.1.call-start
  8.0 0.9 copy.7
  8.9 0.2 fusion.6
  9.1 0.0 copy-done
  9.1 1.5 convolution_convert_fusion
  10.6 0.0 reduce-scatter.2.cloned.1.call-update
  10.6 0.1 convert_reduce_fusion
  10.7 35.5 %all-gather.2.cloned.1.call-done = bf16[128,4096]{1,0:T(8,128)(2,1)} async-done(((bf16[128,1024]{1,0:T(8,128)(2,1)}), bf16[128,4096]{1,0:T(8,128)(2,1)}) %all-gather.2.cloned.1.call-update) | async-done | bytes 1048592 | tf_op jit(solution)/shard_map/all_gather | solution.py:40
  46.2 1.6 fusion
  47.9 1045.5 %all-reduce.2 = (bf16[4096,128]{0,1:T(8,128)(2,1)}, f32[128]{0:T(128)}) all-reduce(f32[4096,128]{0,1:T(8,128)S(1)} %fusion, f32[128]{0:T(128)S(1)} %broadcast_multiply_fusion), channel_id=1, replica_groups=mesh['dx'=16,'dy'=8,'tp'=4] {'dx','dy'}, use_global_device_ids=true, to_apply=%region_1.2 | all-reduce | flops 524416 | bytes 3146752 | tf_op jit(solution)/shard_map/psum | solution.py:53
  1093.4 2.3 copy.8
  1095.6 0.0 reduce-scatter.2.cloned.1.call-done
  (4 shorter events, 0.0 us)
Async XLA Ops:
  7.2 1.9 copy-start
  7.2 39.0 %all-gather.2.cloned.1.call-start = ((), (), s32[]{:S(2)}) async-start(), calls=%async_computation.2 | async-start | bytes 1310720 | tf_op jit(solution)/shard_map/all_gather | solution.py:40
  7.9 1087.7 %reduce-scatter.2.cloned.1.call-start = ((), (), s32[]{:S(2)}) async-start(), calls=%async_computation.1 | async-start | bytes 1310720 | tf_op jit(solution)/shard_map/reduce_scatter | solution.py:50
Sparse Core Ops, SparseCore 0:
  10.1 36.0 all-gather.1
  49.6 31.0 reduce-scatter.1
where the time goes:
time: 1120 us; the launch traced here: 1100 us
  blocking collectives  1050 us (94%)
  waiting for transfers between devices  36.2 us (3%)
  between operations  14.1 us (1%)
    psum x1, blocking collectives, body(): lax.psum((local_weight, local_bias), ('dx', 'dy'))  1050 us
    all_gather x1, waiting for transfers between devices, body(): lax.all_gather(normed, 'tp', axis=1, tiled=True)  35.5 us
  transfers between devices with their start and end apart: 2, of which 1 were waited for; matrix products, arithmetic and copies ran while one was open for 1% of the time, Pallas kernels for 0%

commit v1 on v0

v1 whole, which is shorter than its diff:
```python
import math

import jax
import jax.numpy as jnp
from jax import lax
from jax.experimental import pallas as pl
from jax.experimental.pallas import tpu as pltpu
from jax.sharding import PartitionSpec as P

HD = 128
SEQ = 4096
HEADS = 4
ROWS = 128
WIDE = 1024
HALF = 512
MESH = pl.DeviceIdType.MESH
NEAR = [(kx, kz) for kz in range(2) for kx in range(4) if (kx, kz) != (0, 0)]
NEAR.sort(key=lambda k: -(min(k[0], 4 - k[0]) + k[1]))
ACROSS = [(ky, kc) for ky in (2, 1, 3, 0) for kc in (1, 0) if (ky, kc) != (0, 0)]
FAR = [4, 3, 5, 2, 6, 1, 7]


def rope_back(grad, first_row):
    values = grad.astype(jnp.float32)
    row = lax.broadcasted_iota(jnp.int32, (ROWS, HD), 0)
    lane = lax.broadcasted_iota(jnp.int32, (ROWS, HD), 1)
    positions = ((first_row + row) % SEQ).astype(jnp.float32)
    place = jnp.where(lane < HD // 2, lane, lane - HD // 2).astype(jnp.float32)
    angles = positions * jnp.exp(place * (-2.0 * math.log(1000000.0) / HD))
    sines = jnp.sin(angles)
    sines = jnp.where(lane < HD // 2, sines, -sines)
    return values * jnp.cos(angles) + pltpu.roll(values, HD // 2, 1) * sines


def kernel(
    normed, key_weight, key_grad, input_grad, weight_grad, bias_grad,
    keys, tokens, raw, weights, parts, got, halves, got_far, tile, inputs, bias_near, bias_far,
    load_sem, raw_send, raw_recv, normed_send, normed_recv, weight_send, weight_recv,
    near_send, near_recv, far_send, far_recv, tile_send, tile_recv, wide_send, wide_recv,
    core_send, core_recv, input_send, input_recv, input_own,
    bias_send, bias_recv, bias_far_send, bias_far_recv,
):
    dx, dy, y = lax.axis_index("dx"), lax.axis_index("dy"), lax.axis_index("tp")
    x, c = dy % 4, dx % 2
    z = (dy // 4) * 8 + dx // 2
    zp, zq = z % 2, z // 2
    xz = x * 2 + zp
    group, pair = zq // 2, zq % 2
    other = 1 - c

    def at(x, y, zq, zp, c):
        z = zq * 2 + zp
        return ((z % 8) * 2 + c, (z // 8) * 4 + x, y)

    def remote(source, target, send, recv, device):
        return pltpu.make_async_remote_copy(
            src_ref=source, dst_ref=target, send_sem=send, recv_sem=recv, device_id=device, device_id_type=MESH
        )

    sibling = at(x, y, zq, zp, other)
    barrier = pltpu.get_barrier_semaphore()
    partners = [at(x, y, (zq + k) % 8, zp, c) for k in FAR]
    partners += [at((x + kx) % 4, y, zq, (zp + kz) % 2, c) for kx, kz in NEAR]
    partners += [at(x, (y + ky) % 4, zq, zp, (c + kc) % 2) for ky, kc in ACROSS]
    for partner in partners:
        pl.semaphore_signal(barrier, inc=1, device_id=partner, device_id_type=MESH)

    own_half = pl.ds(pl.multiple_of(c * HALF, HALF), HALF)
    other_half = pl.ds(pl.multiple_of(other * HALF, HALF), HALF)
    own_head = pl.ds(pl.multiple_of(y * HD, HD), HD)
    load_keys = pltpu.make_async_copy(key_grad, keys, load_sem.at[0])
    load_normed = pltpu.make_async_copy(normed.at[:, own_half], tokens.at[c], load_sem.at[1])
    own_rows = pl.ds(pl.multiple_of(y * WIDE + c * HALF, HALF), HALF)
    load_weight = pltpu.make_async_copy(key_weight.at[own_rows], weights.at[:, own_head], load_sem.at[2])
    load_keys.start()
    load_normed.start()
    load_weight.start()
    load_keys.wait()
    first_row = (dx * 8 + dy) * ROWS
    raw[c, :, own_head] = rope_back(keys[...], first_row).astype(jnp.bfloat16)

    pl.semaphore_wait(barrier, len(partners))

    raw_copies = [
        remote(raw.at[c, :, own_head], raw.at[c, :, own_head], raw_send.at[i], raw_recv.at[i],
               at(x, (y + ky) % 4, zq, zp, (c + kc) % 2))
        for i, (ky, kc) in enumerate(ACROSS)
    ]
    for copy in raw_copies:
        copy.start()
    normed_copy = remote(normed.at[:, other_half], tokens.at[c], normed_send, normed_recv, sibling)
    normed_copy.start()
    weight_copies = []
    for i, ky in enumerate((2, 1, 3)):
        there = (y + ky) % 4
        rows = pl.ds(pl.multiple_of(there * WIDE + c * HALF, HALF), HALF)
        weight_copies.append(
            remote(key_weight.at[rows], weights.at[:, own_head], weight_send.at[i], weight_recv.at[i],
                   at(x, there, zq, zp, c))
        )
    for copy in weight_copies:
        copy.start()
    load_normed.wait()
    normed_copy.wait_recv()
    for copy in raw_copies:
        copy.wait_recv()

    product = lax.dot_general(
        tokens[...].reshape(2 * ROWS, HALF), raw[...].reshape(2 * ROWS, HEADS * HD),
        (((0,), (0,)), ((), ())), preferred_element_type=jnp.float32,
    )
    parts[...] = product.astype(jnp.bfloat16).reshape(8, 64, HEADS * HD)
    near_copies = []
    for i, (kx, kz) in enumerate(NEAR):
        there = ((x + kx) % 4) * 2 + (zp + kz) % 2
        near_copies.append(
            remote(parts.at[there], got.at[xz], near_send.at[i], near_recv.at[i],
                   at((x + kx) % 4, y, zq, (zp + kz) % 2, c))
        )
    for copy in near_copies:
        copy.start()
    got[xz] = parts[xz]

    raw_head = raw[:, :, own_head].astype(jnp.float32).reshape(2 * ROWS, HD)
    bias_near[xz] = jnp.broadcast_to(jnp.sum(raw_head, axis=0, keepdims=True), (8, HD))
    bias_copies = [
        remote(bias_near.at[xz], bias_near.at[xz], bias_send.at[i], bias_recv.at[i],
               at((x + kx) % 4, y, zq, (zp + kz) % 2, c))
        for i, (kx, kz) in enumerate(NEAR)
    ]
    for copy in bias_copies:
        copy.start()

    for copy in near_copies:
        copy.wait_recv()
    total = got[0].astype(jnp.float32)
    for s in range(1, 8):
        total += got[s].astype(jnp.float32)
    total = total.astype(jnp.bfloat16)
    for s in range(8):
        halves[s] = total[(s // 2) * 16:(s // 2) * 16 + 16, (s % 2) * 256:(s % 2) * 256 + 256]
    far_copies = [
        remote(halves.at[(zq + k) % 8], got_far.at[zq], far_send.at[i], far_recv.at[i], at(x, y, (zq + k) % 8, zp, c))
        for i, k in enumerate(FAR)
    ]
    for copy in far_copies:
        copy.start()
    got_far[zq] = halves[zq]

    for copy in bias_copies:
        copy.wait()
    bias_part = bias_near[0]
    for s in range(1, 8):
        bias_part += bias_near[s]
    bias_far[zq] = bias_part
    bias_far_copies = [
        remote(bias_far.at[zq], bias_far.at[zq], bias_far_send.at[i], bias_far_recv.at[i],
               at(x, y, (zq + k) % 8, zp, c))
        for i, k in enumerate(FAR)
    ]
    for copy in bias_far_copies:
        copy.start()

    load_weight.wait()
    for copy in weight_copies:
        copy.wait()
    result = lax.dot_general(
        raw[...].reshape(2 * ROWS, HEADS * HD), weights[...],
        (((1,), (1,)), ((), ())), preferred_element_type=jnp.float32,
    )
    inputs[...] = result.astype(jnp.bfloat16).reshape(2, ROWS, HALF)
    input_copy = remote(inputs.at[other], input_grad.at[:, own_half], input_send, input_recv, sibling)
    input_copy.start()
    input_local = pltpu.make_async_copy(inputs.at[c], input_grad.at[:, own_half], input_own)
    input_local.start()

    for copy in far_copies:
        copy.wait_recv()
    final = got_far[0].astype(jnp.float32)
    for s in range(1, 8):
        final += got_far[s].astype(jnp.float32)
    final = (final * (1.0 / 128.0)).astype(jnp.bfloat16)
    tile[0] = final[:, :HD]
    tile[1] = final[:, HD:]

    target = weight_grad.at[y, c, xz, group]
    tile_copies = []
    for k in FAR + [0]:
        for h in range(2):
            i = len(tile_copies)
            there = pair * 2 + h
            tile_copies.append(
                (remote(tile.at[h], target, tile_send.at[i], tile_recv, at(x, there, (zq + k) % 8, zp, c)), k, there)
            )
    own_tiles = [pltpu.make_async_copy(tile.at[h], target, tile_recv) for h in range(2)]
    for copy, k, there in tile_copies:
        if k:
            copy.start()
        else:
            pl.when(there != y)(copy.start)
    for h in range(2):
        pl.when(pair * 2 + h == y)(own_tiles[h].start)

    for copy in bias_far_copies:
        copy.wait()
    bias_all = bias_far[0]
    for s in range(1, 8):
        bias_all += bias_far[s]
    bias_grad[...] = bias_all[0:1] * (1.0 / 128.0)

    own_block = weight_grad.at[:, c, xz]
    pltpu.make_async_copy(own_block, own_block, tile_recv).wait()

    wide_copies = [
        remote(own_block, own_block, wide_send.at[i], wide_recv.at[i], at((x + kx) % 4, y, zq, (zp + kz) % 2, c))
        for i, (kx, kz) in enumerate(NEAR)
    ]
    for copy in wide_copies:
        copy.start()
    core_copies = [remote(own_block, own_block, core_send.at[7], core_recv.at[7], sibling)]
    core_copies[0].start()
    order = sorted(range(7), key=lambda i: -i)
    for i in order:
        kx, kz = NEAR[i]
        came = weight_grad.at[:, c, ((x - kx) % 4) * 2 + (zp - kz) % 2]
        wide_copies[i].wait_recv()
        forward = remote(came, came, core_send.at[i], core_recv.at[i], sibling)
        forward.start()
        core_copies.append(forward)
    for copy in core_copies:
        copy.wait()
    for copy in wide_copies + near_copies + far_copies + raw_copies + [normed_copy]:
        copy.wait_send()
    for copy, k, there in tile_copies:
        if k:
            copy.wait_send()
        else:
            pl.when(there != y)(copy.wait_send)
    input_copy.wait()
    input_local.wait()


def body(normed, key_weight, key_grad):
    dma = pltpu.SemaphoreType.DMA
    bf16, f32 = jnp.bfloat16, jnp.float32
    anywhere = pl.BlockSpec(memory_space=pl.ANY)
    input_grad, weight_grad, bias_grad = pl.pallas_call(
        kernel,
        out_shape=(
            jax.ShapeDtypeStruct((ROWS, WIDE), bf16),
            jax.ShapeDtypeStruct((4, 2, 8, 4, 16, HD), bf16),
            jax.ShapeDtypeStruct((1, HD), f32),
        ),
        in_specs=[anywhere] * 3,
        out_specs=(anywhere, anywhere, pl.BlockSpec(memory_space=pltpu.VMEM)),
        scratch_shapes=[
            pltpu.VMEM((ROWS, HD), bf16),
            pltpu.VMEM((2, ROWS, HALF), bf16),
            pltpu.VMEM((2, ROWS, HEADS * HD), bf16),
            pltpu.VMEM((HALF, HEADS * HD), bf16),
            pltpu.VMEM((8, 64, HEADS * HD), bf16),
            pltpu.VMEM((8, 64, HEADS * HD), bf16),
            pltpu.VMEM((8, 16, 2 * HD), bf16),
            pltpu.VMEM((8, 16, 2 * HD), bf16),
            pltpu.VMEM((2, 16, HD), bf16),
            pltpu.VMEM((2, ROWS, HALF), bf16),
            pltpu.VMEM((8, 8, HD), f32),
            pltpu.VMEM((8, 8, HD), f32),
            dma((3,)), dma((7,)), dma((7,)), dma, dma, dma((3,)), dma((3,)),
            dma((7,)), dma((7,)), dma((7,)), dma((7,)), dma((16,)), dma, dma((7,)), dma((7,)),
            dma((8,)), dma((8,)), dma, dma, dma,
            dma((7,)), dma((7,)), dma((7,)), dma((7,)),
        ],
        compiler_params=pltpu.CompilerParams(collective_id=0, has_side_effects=True, vmem_limit_bytes=32 << 20),
        cost_estimate=pl.CostEstimate(flops=4 * 256 * 512 * 512, bytes_accessed=4 << 20, transcendentals=0),
        name="key_projection_backward",
    )(normed, key_weight, key_grad)
    return input_grad, weight_grad.reshape(4096, HD), bias_grad.reshape(HD)


def solution(mesh):
    placed = (P(("dx", "dy"), "tp"), P(None, "tp"), P(("dx", "dy"), "tp"))
    return jax.shard_map(
        body,
        mesh=mesh,
        in_specs=placed,
        out_specs=(P(("dx", "dy"), "tp"), P(None, "tp"), P("tp")),
        check_vma=False,
    )
```

time: 1120 us -> 62.9 us (0.06); the launches traced: 1100 us -> 62.6 us
  blocking collectives: 1050 us -> 0 us
  Pallas kernels: 0 us -> 56.9 us
  waiting for transfers between devices: 36.2 us -> 0 us
  between operations: 14.1 us -> 0.65 us
    psum x1 -> x0, blocking collectives: 1050 us -> none  [body(): lax.psum((local_weight, local_bias), ('dx', 'dy'))]
    pallas_call x0 -> x1, Pallas kernels: none -> 56.9 us  [body(): pl.pallas_call(kernel, out_shape=(jax.ShapeDtypeStruct((ROWS, WIDE), bf16...]
    all_gather x1 -> x0, waiting for transfers between devices: 35.5 us -> none  [body(): lax.all_gather(normed, 'tp', axis=1, tiled=True)]
  transfers between devices with their start and end apart: 2 -> 0, of which waited for: 1 -> 0; matrix products, arithmetic and copies ran while one was open for 1% -> 0% of each run, Pallas kernels for 0% -> 0%
where the time goes in v1:
time: 62.9 us; the launch traced here: 62.6 us
  Pallas kernels  56.9 us (90%)
  local copies, waits for them, and re-layouts  5.11 us (8%)
  between operations  0.65 us (1%)
    pallas_call x1, Pallas kernels, body(): pl.pallas_call(kernel, out_shape=(jax.ShapeDtypeStruct((ROWS, WIDE), bf16...  56.9 us
    unnamed x9, local copies, waits for them, and re-layouts  5.11 us

profile of v1, /device:TPU:1, one launch (start us, length us, event | category | flops | bytes accessed | tf_op | source)
XLA Modules:
  0.0 62.6 jit_solution(12268143635998272920)
XLA Ops:
  0.6 0.0 copy-start
  0.6 1.2 %copy-done = bf16[4096,128]{1,0:T(8,128)(2,1)S(1)} copy-done((bf16[4096,128]{1,0:T(8,128)(2,1)S(1)}, bf16[4096,128]{1,0:T(8,128)(2,1)}, u32[]{:S(2)}) %copy-start) | copy-done | bytes 1048600
  1.9 0.0 copy-start.1
  1.9 0.9 %copy-done.1 = bf16[128,1024]{1,0:T(8,128)(2,1)S(1)} copy-done((bf16[128,1024]{1,0:T(8,128)(2,1)S(1)}, bf16[128,1024]{1,0:T(8,128)(2,1)}, u32[]{:S(2)}) %copy-start.1) | copy-done | bytes 262168
  2.8 0.0 copy-start.2
  2.8 0.8 %copy-done.2 = bf16[128,128]{1,0:T(8,128)(2,1)S(1)} copy-done((bf16[128,128]{1,0:T(8,128)(2,1)S(1)}, bf16[128,128]{1,0:T(8,128)(2,1)}, u32[]{:S(2)}) %copy-start.2) | copy-done | bytes 32792
  3.6 56.9 %key_projection_backward.1 = (bf16[128,1024]{1,0:T(8,128)(2,1)S(1)}, bf16[4,2,8,4,16,128]{5,4,3,2,1,0:T(8,128)(2,1)S(1)}, f32[1,128]{1,0:T(1,128)S(1)}) custom-call(bf16[128,1024]{1,0:T(8,128)(2,1)S(1)} %copy-done.1, bf16[4096,128]{1,0:T(8,128)(2,1)S(1)} %copy-done, bf16[128,128]{1,0:T(8,128)(2,1)S(1)} %copy-done.2), custom_call_target="tpu_custom_call" | custom-call | flops 268435456 | bytes 4194304 | tf_op jit(solution)/shard_map/key_projection_backward/pallas_call | solution.py:247
  60.5 0.7 %copy.9 = bf16[128,1024]{1,0:T(8,128)(2,1)} copy(bf16[128,1024]{1,0:T(8,128)(2,1)S(1)} %get-tuple-element.12) | data formatting | bytes 524288
  61.2 1.0 %copy.10 = bf16[4096,128]{1,0:T(8,128)(2,1)} copy(bf16[4096,128]{1,0:T(8,128)(2,1)S(1)} %bitcast.2) | data formatting | bytes 2097152
  62.1 0.5 copy.11
Async XLA Ops:
  0.6 1.2 %copy-start = (bf16[4096,128]{1,0:T(8,128)(2,1)S(1)}, bf16[4096,128]{1,0:T(8,128)(2,1)}, u32[]{:S(2)}) copy-start(bf16[4096,128]{1,0:T(8,128)(2,1)} %key_weight.1) | copy-start | bytes 3145732
  1.9 0.9 %copy-start.1 = (bf16[128,1024]{1,0:T(8,128)(2,1)S(1)}, bf16[128,1024]{1,0:T(8,128)(2,1)}, u32[]{:S(2)}) copy-start(bf16[128,1024]{1,0:T(8,128)(2,1)} %normed.1) | copy-start | bytes 786436
  2.8 0.8 %copy-start.2 = (bf16[128,128]{1,0:T(8,128)(2,1)S(1)}, bf16[128,128]{1,0:T(8,128)(2,1)}, u32[]{:S(2)}) copy-start(bf16[128,128]{1,0:T(8,128)(2,1)} %key_grad.1) | copy-start | bytes 98308

commit v2 on v1

v2 whole, which is shorter than its diff:
```python
import math

import jax
import jax.numpy as jnp
from jax import lax
from jax.experimental import pallas as pl
from jax.experimental.pallas import tpu as pltpu
from jax.sharding import PartitionSpec as P

HD = 128
SEQ = 4096
HEADS = 4
ROWS = 128
WIDE = 1024
HALF = 512
MESH = pl.DeviceIdType.MESH
NEAR = [(kx, kz) for kz in range(2) for kx in range(4) if (kx, kz) != (0, 0)]
NEAR.sort(key=lambda k: -(min(k[0], 4 - k[0]) + k[1]))
ACROSS = [(ky, kc) for ky in (2, 1, 3, 0) for kc in (1, 0) if (ky, kc) != (0, 0)]
FAR = [4, 3, 5, 2, 6, 1, 7]
GROUPS = 4


def rope_back(grad, first_row):
    values = grad.astype(jnp.float32)
    row = lax.broadcasted_iota(jnp.int32, (ROWS, HD), 0)
    lane = lax.broadcasted_iota(jnp.int32, (ROWS, HD), 1)
    positions = ((first_row + row) % SEQ).astype(jnp.float32)
    place = jnp.where(lane < HD // 2, lane, lane - HD // 2).astype(jnp.float32)
    angles = positions * jnp.exp(place * (-2.0 * math.log(1000000.0) / HD))
    sines = jnp.sin(angles)
    sines = jnp.where(lane < HD // 2, sines, -sines)
    return values * jnp.cos(angles) + pltpu.roll(values, HD // 2, 1) * sines


def kernel(
    normed, key_weight, key_grad, input_grad, weight_grad, bias_grad,
    keys, tokens, turned, raw, weights, parts, got, halves, got_far, tile, inputs, bias_near, bias_far,
    load_sem, raw_send, raw_recv, normed_send, normed_recv, weight_send, weight_recv,
    near_send, near_recv, far_send, far_recv, tile_send, tile_recv, wide_send, wide_recv,
    core_send, core_recv, input_send, input_recv, input_own,
    bias_send, bias_recv, bias_far_send, bias_far_recv, one_away, two_away,
):
    dx, dy, y = lax.axis_index("dx"), lax.axis_index("dy"), lax.axis_index("tp")
    x, c = dy % 4, dx % 2
    z = (dy // 4) * 8 + dx // 2
    zp, zq = z % 2, z // 2
    xz = x * 2 + zp
    group, pair = zq // 2, zq % 2
    other = 1 - c

    def at(x, y, zq, zp, c):
        z = zq * 2 + zp
        return ((z % 8) * 2 + c, (z // 8) * 4 + x, y)

    def along(k):
        return at(x, y, (zq + k) % 8, zp, c)

    def near(kx, kz):
        return at((x + kx) % 4, y, zq, (zp + kz) % 2, c)

    def signal(semaphore, device):
        pl.semaphore_signal(semaphore, inc=1, device_id=device, device_id_type=MESH)

    def remote(source, target, send, recv, device):
        return pltpu.make_async_remote_copy(
            src_ref=source, dst_ref=target, send_sem=send, recv_sem=recv, device_id=device, device_id_type=MESH
        )

    sibling = at(x, y, zq, zp, other)
    barrier = pltpu.get_barrier_semaphore()
    partners = [along(1), along(7)] + [near(kx, kz) for kx, kz in NEAR]
    partners += [at(x, (y + ky) % 4, zq, zp, (c + kc) % 2) for ky, kc in ACROSS]
    for partner in partners:
        signal(barrier, partner)

    own_half = pl.ds(pl.multiple_of(c * HALF, HALF), HALF)
    other_half = pl.ds(pl.multiple_of(other * HALF, HALF), HALF)
    own_head = pl.ds(pl.multiple_of(y * HD, HD), HD)
    load_keys = pltpu.make_async_copy(key_grad, keys, load_sem.at[0])
    load_normed = pltpu.make_async_copy(normed.at[:, own_half], tokens.at[c], load_sem.at[1])
    own_rows = pl.ds(pl.multiple_of(y * WIDE + c * HALF, HALF), HALF)
    load_weight = pltpu.make_async_copy(key_weight.at[own_rows], weights.at[:, own_head], load_sem.at[2])
    load_keys.start()
    load_normed.start()
    load_weight.start()
    load_keys.wait()
    first_row = (dx * 8 + dy) * ROWS
    raw[c, :, own_head] = rope_back(keys[...], first_row).astype(jnp.bfloat16)

    pl.semaphore_wait(barrier, len(partners))

    raw_copies = [
        remote(raw.at[c, :, own_head], raw.at[c, :, own_head], raw_send.at[i], raw_recv.at[i],
               at(x, (y + ky) % 4, zq, zp, (c + kc) % 2))
        for i, (ky, kc) in enumerate(ACROSS)
    ]
    for copy in raw_copies:
        copy.start()
    normed_copy = remote(normed.at[:, other_half], tokens.at[c], normed_send, normed_recv, sibling)
    normed_copy.start()
    for k in (1, 7):
        signal(one_away, along(k))
    load_normed.wait()
    normed_copy.wait_recv()
    turned[...] = tokens[...].reshape(2 * ROWS, HALF).T
    pl.semaphore_wait(one_away, 2)
    for k in (2, 6):
        signal(two_away, along(k))
    for copy in raw_copies:
        copy.wait_recv()

    product = jnp.dot(
        turned[...], raw[...].reshape(2 * ROWS, HEADS * HD), preferred_element_type=jnp.float32
    )
    parts[...] = product.astype(jnp.bfloat16).reshape(8, GROUPS, 16, HEADS * HD)
    step = 1 + 2 * pair
    order = [(group + 2) % 4, (group + step) % 4, (group + 4 - step) % 4, group]
    near_copies = [
        [
            remote(parts.at[((x + kx) % 4) * 2 + (zp + kz) % 2, g], got.at[xz, g],
                   near_send.at[j, i], near_recv.at[j, i], near(kx, kz))
            for i, (kx, kz) in enumerate(NEAR)
        ]
        for j, g in enumerate(order)
    ]
    for copies in near_copies:
        for copy in copies:
            copy.start()
    got[xz] = parts[xz]

    raw_head = raw[:, :, own_head].astype(jnp.float32).reshape(2 * ROWS, HD)
    bias_near[xz] = jnp.broadcast_to(jnp.sum(raw_head, axis=0, keepdims=True), (8, HD))
    bias_copies = [
        remote(bias_near.at[xz], bias_near.at[xz], bias_send.at[i], bias_recv.at[i], near(kx, kz))
        for i, (kx, kz) in enumerate(NEAR)
    ]
    for copy in bias_copies:
        copy.start()

    pl.semaphore_wait(two_away, 2)
    far_copies = []
    for j, g in enumerate(order):
        for copy in near_copies[j]:
            copy.wait_recv()
        total = got[0, g].astype(jnp.float32)
        for s in range(1, 8):
            total += got[s, g].astype(jnp.float32)
        total = total.astype(jnp.bfloat16)
        for h in range(2):
            halves[g * 2 + h] = total[:, h * 256:h * 256 + 256]
        for h in range(2 if j < 3 else 1):
            there = g * 2 + h if j < 3 else g * 2 + 1 - pair
            copy = remote(halves.at[there], got_far.at[zq], far_send.at[len(far_copies)], far_recv,
                          at(x, y, there, zp, c))
            copy.start()
            far_copies.append(copy)
    got_far[zq] = halves[zq]

    weight_copies = []
    for i, ky in enumerate((2, 1, 3)):
        there = (y + ky) % 4
        rows = pl.ds(pl.multiple_of(there * WIDE + c * HALF, HALF), HALF)
        weight_copies.append(
            remote(key_weight.at[rows], weights.at[:, own_head], weight_send.at[i], weight_recv.at[i],
                   at(x, there, zq, zp, c))
        )
    for copy in weight_copies:
        copy.start()

    for copy in bias_copies:
        copy.wait()
    bias_part = bias_near[0]
    for s in range(1, 8):
        bias_part += bias_near[s]
    bias_far[zq] = bias_part
    bias_far_copies = [
        remote(bias_far.at[zq], bias_far.at[zq], bias_far_send.at[i], bias_far_recv.at[i], along(k))
        for i, k in enumerate(FAR)
    ]
    for copy in bias_far_copies:
        copy.start()

    arrived = got_far.at[pl.ds(0, 7)]
    pltpu.make_async_copy(arrived, arrived, far_recv).wait()
    final = got_far[0].astype(jnp.float32)
    for s in range(1, 8):
        final += got_far[s].astype(jnp.float32)
    final = (final * (1.0 / 128.0)).astype(jnp.bfloat16)
    tile[0] = final[:, :HD]
    tile[1] = final[:, HD:]

    target = weight_grad.at[y, c, xz, group]
    tile_copies = []
    for k in FAR + [0]:
        for h in range(2):
            there = pair * 2 + h
            copy = remote(tile.at[h], target, tile_send.at[len(tile_copies)], tile_recv.at[group],
                          at(x, there, (zq + k) % 8, zp, c))
            tile_copies.append((copy, k, there))
    own_tiles = [pltpu.make_async_copy(tile.at[h], target, tile_recv.at[group]) for h in range(2)]
    for copy, k, there in tile_copies:
        if k:
            copy.start()
        else:
            pl.when(there != y)(copy.start)
    for h in range(2):
        pl.when(pair * 2 + h == y)(own_tiles[h].start)

    load_weight.wait()
    for copy in weight_copies:
        copy.wait_recv()
    result = lax.dot_general(
        raw[...].reshape(2 * ROWS, HEADS * HD), weights[...],
        (((1,), (1,)), ((), ())), preferred_element_type=jnp.float32,
    )
    inputs[...] = result.astype(jnp.bfloat16).reshape(2, ROWS, HALF)
    input_copy = remote(inputs.at[other], input_grad.at[:, own_half], input_send, input_recv, sibling)
    input_copy.start()
    input_local = pltpu.make_async_copy(inputs.at[c], input_grad.at[:, own_half], input_own)
    input_local.start()

    arrivals = [group, (group + 1) % 4, (group + 3) % 4, (group + 2) % 4]
    wide_copies = []
    for j, g in enumerate(arrivals):
        block = weight_grad.at[:, c, xz, g]
        pltpu.make_async_copy(block, block, tile_recv.at[g]).wait()
        copies = [
            remote(block, block, wide_send.at[j, i], wide_recv.at[j, i], near(kx, kz))
            for i, (kx, kz) in enumerate(NEAR)
        ]
        for copy in copies:
            copy.start()
        wide_copies.append(copies)

    for copy in bias_far_copies:
        copy.wait()
    bias_all = bias_far[0]
    for s in range(1, 8):
        bias_all += bias_far[s]
    bias_grad[...] = bias_all[0:1] * (1.0 / 128.0)

    core_copies = []
    for j, g in enumerate(arrivals):
        for copy in wide_copies[j]:
            copy.wait_recv()
        block = weight_grad.at[:, c, :, g]
        copy = remote(block, block, core_send.at[j], core_recv.at[j], sibling)
        copy.start()
        core_copies.append(copy)

    for copy in raw_copies + [normed_copy] + sum(near_copies, []) + far_copies + weight_copies + sum(wide_copies, []):
        copy.wait_send()
    for copy, k, there in tile_copies:
        if k:
            copy.wait_send()
        else:
            pl.when(there != y)(copy.wait_send)
    input_copy.wait()
    input_local.wait()
    for copy in core_copies:
        copy.wait()


def finish(input_vmem, weight_vmem, bias_vmem, input_grad, weight_grad, bias_grad, done):
    copies = [
        pltpu.make_async_copy(weight_vmem, weight_grad, done.at[0]),
        pltpu.make_async_copy(input_vmem, input_grad, done.at[1]),
        pltpu.make_async_copy(bias_vmem, bias_grad, done.at[2]),
    ]
    for copy in copies:
        copy.start()
    for copy in copies:
        copy.wait()


def body(normed, key_weight, key_grad):
    dma, regular = pltpu.SemaphoreType.DMA, pltpu.SemaphoreType.REGULAR
    bf16, f32 = jnp.bfloat16, jnp.float32
    hbm = pl.BlockSpec(memory_space=pltpu.HBM)
    anywhere = pl.BlockSpec(memory_space=pl.ANY)
    local = pl.BlockSpec(memory_space=pltpu.VMEM)
    shapes = (
        jax.ShapeDtypeStruct((ROWS, WIDE), bf16),
        jax.ShapeDtypeStruct((4, 2, 8, GROUPS, 16, HD), bf16),
        jax.ShapeDtypeStruct((1, HD), f32),
    )
    normed, key_weight, key_grad = (pltpu.with_memory_space_constraint(a, pltpu.HBM) for a in (normed, key_weight, key_grad))
    results = pl.pallas_call(
        kernel,
        out_shape=shapes,
        in_specs=[hbm] * 3,
        out_specs=(anywhere, anywhere, local),
        scratch_shapes=[
            pltpu.VMEM((ROWS, HD), bf16),
            pltpu.VMEM((2, ROWS, HALF), bf16),
            pltpu.VMEM((HALF, 2 * ROWS), bf16),
            pltpu.VMEM((2, ROWS, HEADS * HD), bf16),
            pltpu.VMEM((HALF, HEADS * HD), bf16),
            pltpu.VMEM((8, GROUPS, 16, HEADS * HD), bf16),
            pltpu.VMEM((8, GROUPS, 16, HEADS * HD), bf16),
            pltpu.VMEM((8, 16, 2 * HD), bf16),
            pltpu.VMEM((8, 16, 2 * HD), bf16),
            pltpu.VMEM((2, 16, HD), bf16),
            pltpu.VMEM((2, ROWS, HALF), bf16),
            pltpu.VMEM((8, 8, HD), f32),
            pltpu.VMEM((8, 8, HD), f32),
            dma((3,)), dma((7,)), dma((7,)), dma, dma, dma((3,)), dma((3,)),
            dma((4, 7)), dma((4, 7)), dma((7,)), dma, dma((16,)), dma((4,)), dma((4, 7)), dma((4, 7)),
            dma((4,)), dma((4,)), dma, dma, dma,
            dma((7,)), dma((7,)), dma((7,)), dma((7,)), regular, regular,
        ],
        compiler_params=pltpu.CompilerParams(collective_id=0, has_side_effects=True, vmem_limit_bytes=32 << 20),
        cost_estimate=pl.CostEstimate(flops=4 * 256 * 512 * 512, bytes_accessed=4 << 20, transcendentals=0),
        name="key_projection_backward",
    )(normed, key_weight, key_grad)
    input_grad, weight_grad, bias_grad = pl.pallas_call(
        finish,
        out_shape=shapes,
        in_specs=[anywhere] * 3,
        out_specs=(hbm,) * 3,
        scratch_shapes=[dma((3,))],
        name="write_results",
    )(*results)
    return input_grad, weight_grad.reshape(4096, HD), bias_grad.reshape(HD)


def solution(mesh):
    placed = (P(("dx", "dy"), "tp"), P(None, "tp"), P(("dx", "dy"), "tp"))
    return jax.shard_map(
        body,
        mesh=mesh,
        in_specs=placed,
        out_specs=(P(("dx", "dy"), "tp"), P(None, "tp"), P("tp")),
        check_vma=False,
    )
```

time: 62.9 us -> 93.5 us (1.49)
  Pallas kernels: 56.9 us -> 90.5 us
  local copies, waits for them, and re-layouts: 5.11 us -> 2.23 us
    pallas_call x1 -> x2, Pallas kernels: 56.9 us -> 90.5 us  [the longest x1 49.6 us: body(): pl.pallas_call(kernel, out_shape=shapes, in_specs=[hbm] * 3, out_specs=(a...]
    unnamed x9 -> x6, local copies, waits for them, and re-layouts: 5.11 us -> 2.23 us
where the time goes in v2:
time: 93.5 us; the launch traced here: 93.3 us
  Pallas kernels  90.5 us (97%)
  local copies, waits for them, and re-layouts  2.23 us (2%)
    pallas_call x1, Pallas kernels, body(): pl.pallas_call(kernel, out_shape=shapes, in_specs=[hbm] * 3, out_specs=(a...  49.6 us
    pallas_call x1, Pallas kernels, body(): pl.pallas_call(finish, out_shape=shapes, in_specs=[anywhere] * 3, out_spe...  40.8 us
    unnamed x6, local copies, waits for them, and re-layouts  2.23 us

profile of v2, /device:TPU:1, one launch (start us, length us, event | category | flops | bytes accessed | tf_op | source)
XLA Modules:
  0.0 93.3 jit_solution(7133065289078308948)
XLA Ops:
  0.6 49.6 %key_projection_backward.1 = (bf16[128,1024]{1,0:T(8,128)(2,1)S(1)}, bf16[4,2,8,4,16,128]{5,4,3,2,1,0:T(8,128)(2,1)S(1)}, f32[1,128]{1,0:T(1,128)S(1)}) custom-call(bf16[128,1024]{1,0:T(8,128)(2,1)} %normed.1, bf16[4096,128]{1,0:T(8,128)(2,1)} %key_weight.1, bf16[128,128]{1,0:T(8,128)(2,1)} %key_grad.1), custom_call_target="tpu_custom_call" | custom-call | flops 268435456 | bytes 4194304 | tf_op jit(solution)/shard_map/key_projection_backward/pallas_call | solution.py:289
  50.2 0.0 copy-start
  50.3 1.0 %copy-done = bf16[4,2,8,4,16,128]{5,4,3,2,1,0:T(8,128)(2,1)} copy-done((bf16[4,2,8,4,16,128]{5,4,3,2,1,0:T(8,128)(2,1)}, bf16[4,2,8,4,16,128]{5,4,3,2,1,0:T(8,128)(2,1)S(1)}, u32[]{:S(2)}) %copy-start) | copy-done | bytes 1048600
  51.2 0.0 copy-start.1
  51.2 0.7 copy-done.1
  51.9 0.0 copy-start.2
  51.9 0.6 copy-done.2
  52.5 40.8 %write_results.1 = (bf16[128,1024]{1,0:T(8,128)(2,1)}, bf16[4,2,8,4,16,128]{5,4,3,2,1,0:T(8,128)(2,1)}, f32[1,128]{1,0:T(1,128)}) custom-call(bf16[128,1024]{1,0:T(8,128)(2,1)} %copy-done.1, bf16[4,2,8,4,16,128]{5,4,3,2,1,0:T(8,128)(2,1)} %copy-done, f32[1,128]{1,0:T(1,128)} %copy-done.2), custom_call_target="tpu_custom_call" | custom-call | tf_op jit(solution)/shard_map/write_results/pallas_call | solution.py:317
Async XLA Ops:
  50.2 1.0 %copy-start = (bf16[4,2,8,4,16,128]{5,4,3,2,1,0:T(8,128)(2,1)}, bf16[4,2,8,4,16,128]{5,4,3,2,1,0:T(8,128)(2,1)S(1)}, u32[]{:S(2)}) copy-start(bf16[4,2,8,4,16,128]{5,4,3,2,1,0:T(8,128)(2,1)S(1)} %get-tuple-element.10.weight_vmem) | copy-start | bytes 3145732
  51.2 0.7 copy-start.1
  51.9 0.6 copy-start.2

commit v3 on v2

--- a/solution.py
+++ b/solution.py
@@ -320,6 +320,7 @@
         in_specs=[anywhere] * 3,
         out_specs=(hbm,) * 3,
         scratch_shapes=[dma((3,))],
+        compiler_params=pltpu.CompilerParams(vmem_limit_bytes=1 << 20),
         name="write_results",
     )(*results)
     return input_grad, weight_grad.reshape(4096, HD), bias_grad.reshape(HD)

time: 93.5 us -> 51.5 us (0.55)
  Pallas kernels: 90.5 us -> 50.7 us
  local copies, waits for them, and re-layouts: 2.23 us -> 0 us
    pallas_call x1, Pallas kernels: 40.8 us -> 1.08 us  [body(): pl.pallas_call(finish, out_shape=shapes, in_specs=[anywhere] * 3, out_spe...]
    unnamed x6 -> x0, local copies, waits for them, and re-layouts: 2.23 us -> none
where the time goes in v3:
time: 51.5 us; the launch traced here: 51.3 us
  Pallas kernels  50.7 us (98%)
  between operations  0.64 us (1%)
    pallas_call x1, Pallas kernels, body(): pl.pallas_call(kernel, out_shape=shapes, in_specs=[hbm] * 3, out_specs=(a...  49.6 us
    pallas_call x1, Pallas kernels, body(): pl.pallas_call(finish, out_shape=shapes, in_specs=[anywhere] * 3, out_spe...  1.08 us

profile of v3, /device:TPU:1, one launch (start us, length us, event | category | flops | bytes accessed | tf_op | source)
XLA Modules:
  0.0 51.3 jit_solution(3136564381879157362)
XLA Ops:
  0.6 49.6 %key_projection_backward.1 = (bf16[128,1024]{1,0:T(8,128)(2,1)S(1)}, bf16[4,2,8,4,16,128]{5,4,3,2,1,0:T(8,128)(2,1)S(1)}, f32[1,128]{1,0:T(1,128)S(1)}) custom-call(bf16[128,1024]{1,0:T(8,128)(2,1)} %normed.1, bf16[4096,128]{1,0:T(8,128)(2,1)} %key_weight.1, bf16[128,128]{1,0:T(8,128)(2,1)} %key_grad.1), custom_call_target="tpu_custom_call" | custom-call | flops 268435456 | bytes 4194304 | tf_op jit(solution)/shard_map/key_projection_backward/pallas_call | solution.py:289
  50.2 1.1 %write_results.1 = (bf16[128,1024]{1,0:T(8,128)(2,1)}, bf16[4,2,8,4,16,128]{5,4,3,2,1,0:T(8,128)(2,1)}, f32[1,128]{1,0:T(1,128)}) custom-call(bf16[128,1024]{1,0:T(8,128)(2,1)S(1)} %get-tuple-element.9.input_vmem, bf16[4,2,8,4,16,128]{5,4,3,2,1,0:T(8,128)(2,1)S(1)} %get-tuple-element.10.weight_vmem, f32[1,128]{1,0:T(1,128)S(1)} %get-tuple-element.11.bias_vmem), custom_call_target="tpu_custom_call" | custom-call | tf_op jit(solution)/shard_map/write_results/pallas_call | solution.py:317

commit v4 on v3

--- a/solution.py
+++ b/solution.py
@@ -33,13 +33,25 @@
     return values * jnp.cos(angles) + pltpu.roll(values, HD // 2, 1) * sines
 
 
+def split(row):
+    high = row.astype(jnp.bfloat16).astype(jnp.float32)
+    middle = (row - high).astype(jnp.bfloat16).astype(jnp.float32)
+    place = lax.broadcasted_iota(jnp.int32, (16, HD), 0)
+    low = jnp.where(place == 2, row - high - middle, 0.0)
+    return jnp.where(place == 0, high, jnp.where(place == 1, middle, low)).astype(jnp.bfloat16)
+
+
+def joined(tile):
+    return tile[0:1] + tile[1:2] + tile[2:3]
+
+
 def kernel(
     normed, key_weight, key_grad, input_grad, weight_grad, bias_grad,
-    keys, tokens, turned, raw, weights, parts, got, halves, got_far, tile, inputs, bias_near, bias_far,
+    keys, tokens, turned, raw, weights, parts, got, halves, got_far, tile, inputs,
     load_sem, raw_send, raw_recv, normed_send, normed_recv, weight_send, weight_recv,
     near_send, near_recv, far_send, far_recv, tile_send, tile_recv, wide_send, wide_recv,
     core_send, core_recv, input_send, input_recv, input_own,
-    bias_send, bias_recv, bias_far_send, bias_far_recv, one_away, two_away,
+    cross_send, cross_recv, one_away, two_away,
 ):
     dx, dy, y = lax.axis_index("dx"), lax.axis_index("dy"), lax.axis_index("tp")
     x, c = dy % 4, dx % 2
@@ -66,6 +78,9 @@
         return pltpu.make_async_remote_copy(
             src_ref=source, dst_ref=target, send_sem=send, recv_sem=recv, device_id=device, device_id_type=MESH
         )
+
+    def wait_for(buffer, semaphore):
+        pltpu.make_async_copy(buffer, buffer, semaphore).wait()
 
     sibling = at(x, y, zq, zp, other)
     barrier = pltpu.get_barrier_semaphore()
@@ -113,45 +128,42 @@
     product = jnp.dot(
         turned[...], raw[...].reshape(2 * ROWS, HEADS * HD), preferred_element_type=jnp.float32
     )
-    parts[...] = product.astype(jnp.bfloat16).reshape(8, GROUPS, 16, HEADS * HD)
     step = 1 + 2 * pair
     order = [(group + 2) % 4, (group + step) % 4, (group + 4 - step) % 4, group]
-    near_copies = [
-        [
-            remote(parts.at[((x + kx) % 4) * 2 + (zp + kz) % 2, g], got.at[xz, g],
-                   near_send.at[j, i], near_recv.at[j, i], near(kx, kz))
-            for i, (kx, kz) in enumerate(NEAR)
-        ]
-        for j, g in enumerate(order)
-    ]
-    for copies in near_copies:
-        for copy in copies:
+    main = pl.ds(0, HEADS * HD)
+    parts[:, :, :, main] = product.astype(jnp.bfloat16).reshape(8, GROUPS, 16, HEADS * HD)
+    raw_head = raw[:, :, own_head].astype(jnp.float32).reshape(2 * ROWS, HD)
+    bias_part = split(jnp.sum(raw_head, axis=0, keepdims=True))
+    for d in range(8):
+        parts[d, order[0], :, HEADS * HD:] = bias_part
+    near_copies = []
+    for j, g in enumerate(order):
+        lanes = pl.ds(0, HEADS * HD + HD) if j == 0 else main
+        for kx, kz in NEAR:
+            copy = remote(parts.at[((x + kx) % 4) * 2 + (zp + kz) % 2, g, :, lanes], got.at[xz, g, :, lanes],
+                          near_send.at[j], near_recv.at[j], near(kx, kz))
             copy.start()
+            near_copies.append(copy)
     got[xz] = parts[xz]
-
-    raw_head = raw[:, :, own_head].astype(jnp.float32).reshape(2 * ROWS, HD)
-    bias_near[xz] = jnp.broadcast_to(jnp.sum(raw_head, axis=0, keepdims=True), (8, HD))
-    bias_copies = [
-        remote(bias_near.at[xz], bias_near.at[xz], bias_send.at[i], bias_recv.at[i], near(kx, kz))
-        for i, (kx, kz) in enumerate(NEAR)
-    ]
-    for copy in bias_copies:
-        copy.start()
 
     pl.semaphore_wait(two_away, 2)
     far_copies = []
     for j, g in enumerate(order):
-        for copy in near_copies[j]:
-            copy.wait_recv()
-        total = got[0, g].astype(jnp.float32)
+        lanes = pl.ds(0, HEADS * HD + HD) if j == 0 else main
+        wait_for(got.at[pl.ds(0, 7), g, :, lanes], near_recv.at[j])
+        total = got[0, g, :, lanes].astype(jnp.float32)
         for s in range(1, 8):
-            total += got[s, g].astype(jnp.float32)
+            total += got[s, g, :, lanes].astype(jnp.float32)
+        if j == 0:
+            bias_part = split(joined(total[:, HEADS * HD:]))
+            for s in range(8):
+                halves[s, :, 2 * HD:] = bias_part
         total = total.astype(jnp.bfloat16)
         for h in range(2):
-            halves[g * 2 + h] = total[:, h * 256:h * 256 + 256]
+            halves[g * 2 + h, :, :2 * HD] = total[:, h * 256:h * 256 + 256]
         for h in range(2 if j < 3 else 1):
             there = g * 2 + h if j < 3 else g * 2 + 1 - pair
-            copy = remote(halves.at[there], got_far.at[zq], far_send.at[len(far_copies)], far_recv,
+            copy = remote(halves.at[there], got_far.at[zq], far_send, far_recv,
                           at(x, y, there, zp, c))
             copy.start()
             far_copies.append(copy)
@@ -168,25 +180,12 @@
     for copy in weight_copies:
         copy.start()
 
-    for copy in bias_copies:
-        copy.wait()
-    bias_part = bias_near[0]
-    for s in range(1, 8):
-        bias_part += bias_near[s]
-    bias_far[zq] = bias_part
-    bias_far_copies = [
-        remote(bias_far.at[zq], bias_far.at[zq], bias_far_send.at[i], bias_far_recv.at[i], along(k))
-        for i, k in enumerate(FAR)
-    ]
-    for copy in bias_far_copies:
-        copy.start()
-
-    arrived = got_far.at[pl.ds(0, 7)]
-    pltpu.make_async_copy(arrived, arrived, far_recv).wait()
+    wait_for(got_far.at[pl.ds(0, 7)], far_recv)
     final = got_far[0].astype(jnp.float32)
     for s in range(1, 8):
         final += got_far[s].astype(jnp.float32)
-    final = (final * (1.0 / 128.0)).astype(jnp.bfloat16)
+    bias_grad[...] = joined(final[:, 2 * HD:]) * (1.0 / 128.0)
+    final = (final[:, :2 * HD] * (1.0 / 128.0)).astype(jnp.bfloat16)
     tile[0] = final[:, :HD]
     tile[1] = final[:, HD:]
 
@@ -220,46 +219,45 @@
     input_local = pltpu.make_async_copy(inputs.at[c], input_grad.at[:, own_half], input_own)
     input_local.start()
 
+    for copy in raw_copies + [normed_copy] + weight_copies:
+        copy.wait_send()
+    for j in range(GROUPS):
+        lanes = pl.ds(0, HEADS * HD + HD) if j == 0 else main
+        wait_for(parts.at[pl.ds(0, 7), 0, :, lanes], near_send.at[j])
+    wait_for(halves.at[pl.ds(0, 7)], far_send)
+
     arrivals = [group, (group + 1) % 4, (group + 3) % 4, (group + 2) % 4]
-    wide_copies = []
+    last = GROUPS - 1
     for j, g in enumerate(arrivals):
         block = weight_grad.at[:, c, xz, g]
-        pltpu.make_async_copy(block, block, tile_recv.at[g]).wait()
-        copies = [
-            remote(block, block, wide_send.at[j, i], wide_recv.at[j, i], near(kx, kz))
-            for i, (kx, kz) in enumerate(NEAR)
-        ]
-        for copy in copies:
-            copy.start()
-        wide_copies.append(copies)
-
-    for copy in bias_far_copies:
-        copy.wait()
-    bias_all = bias_far[0]
-    for s in range(1, 8):
-        bias_all += bias_far[s]
-    bias_grad[...] = bias_all[0:1] * (1.0 / 128.0)
-
-    core_copies = []
-    for j, g in enumerate(arrivals):
-        for copy in wide_copies[j]:
-            copy.wait_recv()
-        block = weight_grad.at[:, c, :, g]
-        copy = remote(block, block, core_send.at[j], core_recv.at[j], sibling)
-        copy.start()
-        core_copies.append(copy)
-
-    for copy in raw_copies + [normed_copy] + sum(near_copies, []) + far_copies + weight_copies + sum(wide_copies, []):
-        copy.wait_send()
+        wait_for(block, tile_recv.at[g])
+        for kx, kz in NEAR:
+            if j == last:
+                there = at((x + kx) % 4, y, zq, (zp + kz) % 2, other)
+                remote(block, block, cross_send, cross_recv, there).start()
+            remote(block, block, wide_send.at[j], wide_recv.at[j], near(kx, kz)).start()
+        if j == last:
+            remote(block, block, cross_send, cross_recv, sibling).start()
     for copy, k, there in tile_copies:
         if k:
             copy.wait_send()
         else:
             pl.when(there != y)(copy.wait_send)
+    for j, g in enumerate(arrivals[:last]):
+        wait_for(weight_grad.at[:, c, pl.ds(0, 7), g], wide_recv.at[j])
+        block = weight_grad.at[:, c, :, g]
+        remote(block, block, core_send.at[j], core_recv.at[j], sibling).start()
+    for j, g in enumerate(arrivals):
+        wait_for(weight_grad.at[:, c, pl.ds(0, 7), g], wide_send.at[j])
     input_copy.wait()
     input_local.wait()
-    for copy in core_copies:
-        copy.wait()
+    for j, g in enumerate(arrivals[:last]):
+        wait_for(weight_grad.at[:, c, :, g], core_send.at[j])
+        wait_for(weight_grad.at[:, other, :, g], core_recv.at[j])
+    far = arrivals[last]
+    wait_for(weight_grad.at[:, c, :, far], cross_send)
+    wait_for(weight_grad.at[:, c, pl.ds(0, 7), far], wide_recv.at[last])
+    wait_for(weight_grad.at[:, other, :, far], cross_recv)
 
 
 def finish(input_vmem, weight_vmem, bias_vmem, input_grad, weight_grad, bias_grad, done):
@@ -297,18 +295,16 @@
             pltpu.VMEM((HALF, 2 * ROWS), bf16),
             pltpu.VMEM((2, ROWS, HEADS * HD), bf16),
             pltpu.VMEM((HALF, HEADS * HD), bf16),
-            pltpu.VMEM((8, GROUPS, 16, HEADS * HD), bf16),
-            pltpu.VMEM((8, GROUPS, 16, HEADS * HD), bf16),
-            pltpu.VMEM((8, 16, 2 * HD), bf16),
-            pltpu.VMEM((8, 16, 2 * HD), bf16),
+            pltpu.VMEM((8, GROUPS, 16, HEADS * HD + HD), bf16),
+            pltpu.VMEM((8, GROUPS, 16, HEADS * HD + HD), bf16),
+            pltpu.VMEM((8, 16, 3 * HD), bf16),
+            pltpu.VMEM((8, 16, 3 * HD), bf16),
             pltpu.VMEM((2, 16, HD), bf16),
             pltpu.VMEM((2, ROWS, HALF), bf16),
-            pltpu.VMEM((8, 8, HD), f32),
-            pltpu.VMEM((8, 8, HD), f32),
             dma((3,)), dma((7,)), dma((7,)), dma, dma, dma((3,)), dma((3,)),
-            dma((4, 7)), dma((4, 7)), dma((7,)), dma, dma((16,)), dma((4,)), dma((4, 7)), dma((4, 7)),
-            dma((4,)), dma((4,)), dma, dma, dma,
-            dma((7,)), dma((7,)), dma((7,)), dma((7,)), regular, regular,
+            dma((4,)), dma((4,)), dma, dma, dma((16,)), dma((4,)), dma((4,)), dma((4,)),
+            dma((3,)), dma((3,)), dma, dma, dma,
+            dma, dma, regular, regular,
         ],
         compiler_params=pltpu.CompilerParams(collective_id=0, has_side_effects=True, vmem_limit_bytes=32 << 20),
         cost_estimate=pl.CostEstimate(flops=4 * 256 * 512 * 512, bytes_accessed=4 << 20, transcendentals=0),

time: 51.5 us -> 49.7 us (0.965)
  Pallas kernels: 50.7 us -> 48.9 us
    pallas_call x1, Pallas kernels: 49.6 us -> 47.8 us  [body(): pl.pallas_call(kernel, out_shape=shapes, in_specs=[hbm] * 3, out_specs=(a...]
where the time goes in v4:
time: 49.7 us; the launch traced here: 49.5 us
  Pallas kernels  48.9 us (98%)
  between operations  0.64 us (1%)
    pallas_call x1, Pallas kernels, body(): pl.pallas_call(kernel, out_shape=shapes, in_specs=[hbm] * 3, out_specs=(a...  47.8 us
    pallas_call x1, Pallas kernels, body(): pl.pallas_call(finish, out_shape=shapes, in_specs=[anywhere] * 3, out_spe...  1.08 us

profile of v4, /device:TPU:1, one launch (start us, length us, event | category | flops | bytes accessed | tf_op | source)
XLA Modules:
  0.0 49.5 jit_solution(8290557851759458153)
XLA Ops:
  0.6 47.8 %key_projection_backward.1 = (bf16[128,1024]{1,0:T(8,128)(2,1)S(1)}, bf16[4,2,8,4,16,128]{5,4,3,2,1,0:T(8,128)(2,1)S(1)}, f32[1,128]{1,0:T(1,128)S(1)}) custom-call(bf16[128,1024]{1,0:T(8,128)(2,1)} %normed.1, bf16[4096,128]{1,0:T(8,128)(2,1)} %key_weight.1, bf16[128,128]{1,0:T(8,128)(2,1)} %key_grad.1), custom_call_target="tpu_custom_call" | custom-call | flops 268435456 | bytes 4194304 | tf_op jit(solution)/shard_map/key_projection_backward/pallas_call | solution.py:287
  48.5 1.1 %write_results.1 = (bf16[128,1024]{1,0:T(8,128)(2,1)}, bf16[4,2,8,4,16,128]{5,4,3,2,1,0:T(8,128)(2,1)}, f32[1,128]{1,0:T(1,128)}) custom-call(bf16[128,1024]{1,0:T(8,128)(2,1)S(1)} %get-tuple-element.9.input_vmem, bf16[4,2,8,4,16,128]{5,4,3,2,1,0:T(8,128)(2,1)S(1)} %get-tuple-element.10.weight_vmem, f32[1,128]{1,0:T(1,128)S(1)} %get-tuple-element.11.bias_vmem), custom_call_target="tpu_custom_call" | custom-call | tf_op jit(solution)/shard_map/write_results/pallas_call | solution.py:313

commit v5 on v4

--- a/solution.py
+++ b/solution.py
@@ -33,25 +33,13 @@
     return values * jnp.cos(angles) + pltpu.roll(values, HD // 2, 1) * sines
 
 
-def split(row):
-    high = row.astype(jnp.bfloat16).astype(jnp.float32)
-    middle = (row - high).astype(jnp.bfloat16).astype(jnp.float32)
-    place = lax.broadcasted_iota(jnp.int32, (16, HD), 0)
-    low = jnp.where(place == 2, row - high - middle, 0.0)
-    return jnp.where(place == 0, high, jnp.where(place == 1, middle, low)).astype(jnp.bfloat16)
-
-
-def joined(tile):
-    return tile[0:1] + tile[1:2] + tile[2:3]
-
-
 def kernel(
     normed, key_weight, key_grad, input_grad, weight_grad, bias_grad,
-    keys, tokens, turned, raw, weights, parts, got, halves, got_far, tile, inputs,
+    keys, tokens, turned, raw, weights, parts, got, halves, got_far, tile, inputs, bias_near, bias_far,
     load_sem, raw_send, raw_recv, normed_send, normed_recv, weight_send, weight_recv,
     near_send, near_recv, far_send, far_recv, tile_send, tile_recv, wide_send, wide_recv,
     core_send, core_recv, input_send, input_recv, input_own,
-    cross_send, cross_recv, one_away, two_away,
+    cross_send, cross_recv, bias_send, bias_recv, one_away, two_away,
 ):
     dx, dy, y = lax.axis_index("dx"), lax.axis_index("dy"), lax.axis_index("tp")
     x, c = dy % 4, dx % 2
@@ -84,8 +72,9 @@
 
     sibling = at(x, y, zq, zp, other)
     barrier = pltpu.get_barrier_semaphore()
-    partners = [along(1), along(7)] + [near(kx, kz) for kx, kz in NEAR]
-    partners += [at(x, (y + ky) % 4, zq, zp, (c + kc) % 2) for ky, kc in ACROSS]
+    partners = [at(x, (y + ky) % 4, zq, zp, (c + kc) % 2) for ky, kc in ACROSS]
+    partners += [near(kx, 0) for kx in (2, 1, 3)] + [near(0, 1), along(1), along(7)]
+    partners += [at(x, y, (zq + k) % 8, 1 - zp, c) for k in (1, 7)]
     for partner in partners:
         signal(barrier, partner)
 
@@ -118,56 +107,55 @@
         signal(one_away, along(k))
     load_normed.wait()
     normed_copy.wait_recv()
-    turned[...] = tokens[...].reshape(2 * ROWS, HALF).T
+    turned[...] = tokens[...].reshape(2 * ROWS, HALF).T.reshape(8, GROUPS, 16, 2 * ROWS)
     pl.semaphore_wait(one_away, 2)
     for k in (2, 6):
         signal(two_away, along(k))
-    for copy in raw_copies:
-        copy.wait_recv()
-
-    product = jnp.dot(
-        turned[...], raw[...].reshape(2 * ROWS, HEADS * HD), preferred_element_type=jnp.float32
-    )
+    raw_copies[-1].wait_recv()
     step = 1 + 2 * pair
     order = [(group + 2) % 4, (group + step) % 4, (group + 4 - step) % 4, group]
-    main = pl.ds(0, HEADS * HD)
-    parts[:, :, :, main] = product.astype(jnp.bfloat16).reshape(8, GROUPS, 16, HEADS * HD)
     raw_head = raw[:, :, own_head].astype(jnp.float32).reshape(2 * ROWS, HD)
-    bias_part = split(jnp.sum(raw_head, axis=0, keepdims=True))
-    for d in range(8):
-        parts[d, order[0], :, HEADS * HD:] = bias_part
-    near_copies = []
+    bias_near[x] = jnp.sum(raw_head, axis=0, keepdims=True)
+    for copy in raw_copies[:-1]:
+        copy.wait_recv()
+
     for j, g in enumerate(order):
-        lanes = pl.ds(0, HEADS * HD + HD) if j == 0 else main
-        for kx, kz in NEAR:
-            copy = remote(parts.at[((x + kx) % 4) * 2 + (zp + kz) % 2, g, :, lanes], got.at[xz, g, :, lanes],
-                          near_send.at[j], near_recv.at[j], near(kx, kz))
-            copy.start()
-            near_copies.append(copy)
-    got[xz] = parts[xz]
+        product = jnp.dot(
+            turned[:, g].reshape(8 * 16, 2 * ROWS), raw[...].reshape(2 * ROWS, HEADS * HD),
+            preferred_element_type=jnp.float32,
+        )
+        parts[:, g] = product.astype(jnp.bfloat16).reshape(8, 16, HEADS * HD)
+        for kx in (2, 1, 3):
+            remote(parts.at[pl.ds(((x + kx) % 4) * 2, 2), g], got.at[x, :, g],
+                   near_send.at[j], near_recv.at[j], near(kx, 0)).start()
+        if j == 0:
+            for kx in (2, 1, 3):
+                remote(bias_near.at[x], bias_near.at[x], bias_send.at[0], bias_recv.at[0], near(kx, 0)).start()
+    got[x] = parts[pl.ds(x * 2, 2)]
 
     pl.semaphore_wait(two_away, 2)
-    far_copies = []
     for j, g in enumerate(order):
-        lanes = pl.ds(0, HEADS * HD + HD) if j == 0 else main
-        wait_for(got.at[pl.ds(0, 7), g, :, lanes], near_recv.at[j])
-        total = got[0, g, :, lanes].astype(jnp.float32)
-        for s in range(1, 8):
-            total += got[s, g, :, lanes].astype(jnp.float32)
-        if j == 0:
-            bias_part = split(joined(total[:, HEADS * HD:]))
-            for s in range(8):
-                halves[s, :, 2 * HD:] = bias_part
+        wait_for(got.at[pl.ds(0, 3), :, g], near_recv.at[j])
+        total = got[0, :, g].astype(jnp.float32)
+        for s in range(1, 4):
+            total += got[s, :, g].astype(jnp.float32)
         total = total.astype(jnp.bfloat16)
         for h in range(2):
-            halves[g * 2 + h, :, :2 * HD] = total[:, h * 256:h * 256 + 256]
-        for h in range(2 if j < 3 else 1):
-            there = g * 2 + h if j < 3 else g * 2 + 1 - pair
-            copy = remote(halves.at[there], got_far.at[zq], far_send, far_recv,
-                          at(x, y, there, zp, c))
-            copy.start()
-            far_copies.append(copy)
-    got_far[zq] = halves[zq]
+            for p in range(2):
+                halves[(g * 2 + h) * 2 + p] = total[p, :, h * 256:h * 256 + 256]
+        for h, p in ((pair, 1 - zp), (pair, zp), (1 - pair, zp), (1 - pair, 1 - zp)):
+            if j == 3 and h is pair and p is zp:
+                continue
+            there = g * 2 + h
+            remote(halves.at[there * 2 + p], got_far.at[z], far_send, far_recv, at(x, y, there, p, c)).start()
+        if j == 0:
+            wait_for(bias_near.at[pl.ds(0, 3)], bias_recv.at[0])
+            bias_far[z] = bias_near[0] + bias_near[1] + bias_near[2] + bias_near[3]
+            for k in (8, 7, 9, 6, 10, 5, 11, 4, 12, 3, 13, 2, 14, 1, 15):
+                there = (z + k) % 16
+                remote(bias_far.at[z], bias_far.at[z], bias_send.at[1], bias_recv.at[1],
+                       at(x, y, there // 2, there % 2, c)).start()
+    got_far[z] = halves[z]
 
     weight_copies = []
     for i, ky in enumerate((2, 1, 3)):
@@ -180,12 +168,11 @@
     for copy in weight_copies:
         copy.start()
 
-    wait_for(got_far.at[pl.ds(0, 7)], far_recv)
+    wait_for(got_far.at[pl.ds(0, 15)], far_recv)
     final = got_far[0].astype(jnp.float32)
-    for s in range(1, 8):
+    for s in range(1, 16):
         final += got_far[s].astype(jnp.float32)
-    bias_grad[...] = joined(final[:, 2 * HD:]) * (1.0 / 128.0)
-    final = (final[:, :2 * HD] * (1.0 / 128.0)).astype(jnp.bfloat16)
+    final = (final * (1.0 / 128.0)).astype(jnp.bfloat16)
     tile[0] = final[:, :HD]
     tile[1] = final[:, HD:]
 
@@ -206,6 +193,12 @@
     for h in range(2):
         pl.when(pair * 2 + h == y)(own_tiles[h].start)
 
+    wait_for(bias_far.at[pl.ds(0, 15)], bias_recv.at[1])
+    bias_all = bias_far[0]
+    for s in range(1, 16):
+        bias_all += bias_far[s]
+    bias_grad[...] = bias_all * (1.0 / 128.0)
+
     load_weight.wait()
     for copy in weight_copies:
         copy.wait_recv()
@@ -222,9 +215,10 @@
     for copy in raw_copies + [normed_copy] + weight_copies:
         copy.wait_send()
     for j in range(GROUPS):
-        lanes = pl.ds(0, HEADS * HD + HD) if j == 0 else main
-        wait_for(parts.at[pl.ds(0, 7), 0, :, lanes], near_send.at[j])
-    wait_for(halves.at[pl.ds(0, 7)], far_send)
+        wait_for(parts.at[pl.ds(0, 6), 0], near_send.at[j])
+    wait_for(halves.at[pl.ds(0, 15)], far_send)
+    wait_for(bias_near.at[pl.ds(0, 3)], bias_send.at[0])
+    wait_for(bias_far.at[pl.ds(0, 15)], bias_send.at[1])
 
     arrivals = [group, (group + 1) % 4, (group + 3) % 4, (group + 2) % 4]
     last = GROUPS - 1
@@ -292,19 +286,21 @@
         scratch_shapes=[
             pltpu.VMEM((ROWS, HD), bf16),
             pltpu.VMEM((2, ROWS, HALF), bf16),
-            pltpu.VMEM((HALF, 2 * ROWS), bf16),
+            pltpu.VMEM((8, GROUPS, 16, 2 * ROWS), bf16),
             pltpu.VMEM((2, ROWS, HEADS * HD), bf16),
             pltpu.VMEM((HALF, HEADS * HD), bf16),
-            pltpu.VMEM((8, GROUPS, 16, HEADS * HD + HD), bf16),
-            pltpu.VMEM((8, GROUPS, 16, HEADS * HD + HD), bf16),
-            pltpu.VMEM((8, 16, 3 * HD), bf16),
-            pltpu.VMEM((8, 16, 3 * HD), bf16),
+            pltpu.VMEM((8, GROUPS, 16, HEADS * HD), bf16),
+            pltpu.VMEM((4, 2, GROUPS, 16, HEADS * HD), bf16),
+            pltpu.VMEM((16, 16, 2 * HD), bf16),
+            pltpu.VMEM((16, 16, 2 * HD), bf16),
             pltpu.VMEM((2, 16, HD), bf16),
             pltpu.VMEM((2, ROWS, HALF), bf16),
+            pltpu.VMEM((4, 1, HD), f32),
+            pltpu.VMEM((16, 1, HD), f32),
             dma((3,)), dma((7,)), dma((7,)), dma, dma, dma((3,)), dma((3,)),
             dma((4,)), dma((4,)), dma, dma, dma((16,)), dma((4,)), dma((4,)), dma((4,)),
             dma((3,)), dma((3,)), dma, dma, dma,
-            dma, dma, regular, regular,
+            dma, dma, dma((2,)), dma((2,)), regular, regular,
         ],
         compiler_params=pltpu.CompilerParams(collective_id=0, has_side_effects=True, vmem_limit_bytes=32 << 20),
         cost_estimate=pl.CostEstimate(flops=4 * 256 * 512 * 512, bytes_accessed=4 << 20, transcendentals=0),

time: 49.7 us -> 48.7 us (0.980)
  Pallas kernels: 48.9 us -> 47.9 us
    pallas_call x1, Pallas kernels: 47.8 us -> 46.8 us  [body(): pl.pallas_call(kernel, out_shape=shapes, in_specs=[hbm] * 3, out_specs=(a...]
where the time goes in v5:
time: 48.7 us; the launch traced here: 48.5 us
  Pallas kernels  47.9 us (98%)
  between operations  0.64 us (1%)
    pallas_call x1, Pallas kernels, body(): pl.pallas_call(kernel, out_shape=shapes, in_specs=[hbm] * 3, out_specs=(a...  46.8 us
    pallas_call x1, Pallas kernels, body(): pl.pallas_call(finish, out_shape=shapes, in_specs=[anywhere] * 3, out_spe...  1.08 us

profile of v5, /device:TPU:1, one launch (start us, length us, event | category | flops | bytes accessed | tf_op | source)
XLA Modules:
  0.0 48.5 jit_solution(17338869019816749906)
XLA Ops:
  0.6 46.8 %key_projection_backward.1 = (bf16[128,1024]{1,0:T(8,128)(2,1)S(1)}, bf16[4,2,8,4,16,128]{5,4,3,2,1,0:T(8,128)(2,1)S(1)}, f32[1,128]{1,0:T(1,128)S(1)}) custom-call(bf16[128,1024]{1,0:T(8,128)(2,1)} %normed.1, bf16[4096,128]{1,0:T(8,128)(2,1)} %key_weight.1, bf16[128,128]{1,0:T(8,128)(2,1)} %key_grad.1), custom_call_target="tpu_custom_call" | custom-call | flops 268435456 | bytes 4194304 | tf_op jit(solution)/shard_map/key_projection_backward/pallas_call | solution.py:281
  47.5 1.1 %write_results.1 = (bf16[128,1024]{1,0:T(8,128)(2,1)}, bf16[4,2,8,4,16,128]{5,4,3,2,1,0:T(8,128)(2,1)}, f32[1,128]{1,0:T(1,128)}) custom-call(bf16[128,1024]{1,0:T(8,128)(2,1)S(1)} %get-tuple-element.9.input_vmem, bf16[4,2,8,4,16,128]{5,4,3,2,1,0:T(8,128)(2,1)S(1)} %get-tuple-element.10.weight_vmem, f32[1,128]{1,0:T(1,128)S(1)} %get-tuple-element.11.bias_vmem), custom_call_target="tpu_custom_call" | custom-call | tf_op jit(solution)/shard_map/write_results/pallas_call | solution.py:309

commit v6 on v5

--- a/solution.py
+++ b/solution.py
@@ -119,15 +119,19 @@
     for copy in raw_copies[:-1]:
         copy.wait_recv()
 
+    first_columns = [pl.ds(pl.multiple_of(h * 2 * HD, 2 * HD), 2 * HD) for h in (pair, 1 - pair)]
+
     for j, g in enumerate(order):
         product = jnp.dot(
             turned[:, g].reshape(8 * 16, 2 * ROWS), raw[...].reshape(2 * ROWS, HEADS * HD),
             preferred_element_type=jnp.float32,
         )
         parts[:, g] = product.astype(jnp.bfloat16).reshape(8, 16, HEADS * HD)
-        for kx in (2, 1, 3):
-            remote(parts.at[pl.ds(((x + kx) % 4) * 2, 2), g], got.at[x, :, g],
-                   near_send.at[j], near_recv.at[j], near(kx, 0)).start()
+        for h, columns in enumerate(first_columns if j == 0 else [pl.ds(0, HEADS * HD)]):
+            i = h if j == 0 else j + 1
+            for kx in (2, 1, 3):
+                remote(parts.at[pl.ds(((x + kx) % 4) * 2, 2), g, :, columns], got.at[x, :, g, :, columns],
+                       near_send.at[i], near_recv.at[i], near(kx, 0)).start()
         if j == 0:
             for kx in (2, 1, 3):
                 remote(bias_near.at[x], bias_near.at[x], bias_send.at[0], bias_recv.at[0], near(kx, 0)).start()
@@ -135,19 +139,29 @@
 
     pl.semaphore_wait(two_away, 2)
     for j, g in enumerate(order):
-        wait_for(got.at[pl.ds(0, 3), :, g], near_recv.at[j])
-        total = got[0, :, g].astype(jnp.float32)
-        for s in range(1, 4):
-            total += got[s, :, g].astype(jnp.float32)
-        total = total.astype(jnp.bfloat16)
-        for h in range(2):
-            for p in range(2):
-                halves[(g * 2 + h) * 2 + p] = total[p, :, h * 256:h * 256 + 256]
-        for h, p in ((pair, 1 - zp), (pair, zp), (1 - pair, zp), (1 - pair, 1 - zp)):
-            if j == 3 and h is pair and p is zp:
-                continue
-            there = g * 2 + h
-            remote(halves.at[there * 2 + p], got_far.at[z], far_send, far_recv, at(x, y, there, p, c)).start()
+        if j == 0:
+            for i, (h, columns) in enumerate(zip((pair, 1 - pair), first_columns)):
+                wait_for(got.at[pl.ds(0, 3), :, g, :, columns], near_recv.at[i])
+                total = got[0, :, g, :, columns].astype(jnp.float32)
+                for s in range(1, 4):
+                    total += got[s, :, g, :, columns].astype(jnp.float32)
+                there = g * 2 + h
+                halves[pl.ds(there * 2, 2)] = total.astype(jnp.bfloat16)
+                for p in (1 - zp, zp):
+                    remote(halves.at[there * 2 + p], got_far.at[z], far_send, far_recv, at(x, y, there, p, c)).start()
+        else:
+            wait_for(got.at[pl.ds(0, 3), :, g], near_recv.at[j + 1])
+            total = got[0, :, g].astype(jnp.float32)
+            for s in range(1, 4):
+                total += got[s, :, g].astype(jnp.float32)
+            total = total.astype(jnp.bfloat16)
+            for h in range(2):
+                halves[pl.ds((g * 2 + h) * 2, 2)] = total[:, :, h * 256:h * 256 + 256]
+            for h, p in ((pair, 1 - zp), (pair, zp), (1 - pair, zp), (1 - pair, 1 - zp)):
+                if j == 3 and h is pair and p is zp:
+                    continue
+                there = g * 2 + h
+                remote(halves.at[there * 2 + p], got_far.at[z], far_send, far_recv, at(x, y, there, p, c)).start()
         if j == 0:
             wait_for(bias_near.at[pl.ds(0, 3)], bias_recv.at[0])
             bias_far[z] = bias_near[0] + bias_near[1] + bias_near[2] + bias_near[3]
@@ -214,13 +228,15 @@
 
     for copy in raw_copies + [normed_copy] + weight_copies:
         copy.wait_send()
-    for j in range(GROUPS):
-        wait_for(parts.at[pl.ds(0, 6), 0], near_send.at[j])
+    for i in range(2):
+        wait_for(parts.at[pl.ds(0, 6), 0, :, first_columns[i]], near_send.at[i])
+    for j in range(1, GROUPS):
+        wait_for(parts.at[pl.ds(0, 6), 0], near_send.at[j + 1])
     wait_for(halves.at[pl.ds(0, 15)], far_send)
     wait_for(bias_near.at[pl.ds(0, 3)], bias_send.at[0])
     wait_for(bias_far.at[pl.ds(0, 15)], bias_send.at[1])
 
-    arrivals = [group, (group + 1) % 4, (group + 3) % 4, (group + 2) % 4]
+    arrivals = [group, (group + 4 - step) % 4, (group + step) % 4, (group + 2) % 4]
     last = GROUPS - 1
     for j, g in enumerate(arrivals):
         block = weight_grad.at[:, c, xz, g]
@@ -298,7 +314,7 @@
             pltpu.VMEM((4, 1, HD), f32),
             pltpu.VMEM((16, 1, HD), f32),
             dma((3,)), dma((7,)), dma((7,)), dma, dma, dma((3,)), dma((3,)),
-            dma((4,)), dma((4,)), dma, dma, dma((16,)), dma((4,)), dma((4,)), dma((4,)),
+            dma((5,)), dma((5,)), dma, dma, dma((16,)), dma((4,)), dma((4,)), dma((4,)),
             dma((3,)), dma((3,)), dma, dma, dma,
             dma, dma, dma((2,)), dma((2,)), regular, regular,
         ],

time: 48.7 us -> 48.2 us (0.990)
  Pallas kernels: 47.9 us -> 47.4 us
    pallas_call x1, Pallas kernels: 46.8 us -> 46.3 us  [body(): pl.pallas_call(kernel, out_shape=shapes, in_specs=[hbm] * 3, out_specs=(a...]
where the time goes in v6:
time: 48.2 us; the launch traced here: 48 us
  Pallas kernels  47.4 us (98%)
  between operations  0.64 us (1%)
    pallas_call x1, Pallas kernels, body(): pl.pallas_call(kernel, out_shape=shapes, in_specs=[hbm] * 3, out_specs=(a...  46.3 us
    pallas_call x1, Pallas kernels, body(): pl.pallas_call(finish, out_shape=shapes, in_specs=[anywhere] * 3, out_spe...  1.08 us

profile of v6, /device:TPU:1, one launch (start us, length us, event | category | flops | bytes accessed | tf_op | source)
XLA Modules:
  0.0 48.0 jit_solution(14649497743854049410)
XLA Ops:
  0.6 46.3 %key_projection_backward.1 = (bf16[128,1024]{1,0:T(8,128)(2,1)S(1)}, bf16[4,2,8,4,16,128]{5,4,3,2,1,0:T(8,128)(2,1)S(1)}, f32[1,128]{1,0:T(1,128)S(1)}) custom-call(bf16[128,1024]{1,0:T(8,128)(2,1)} %normed.1, bf16[4096,128]{1,0:T(8,128)(2,1)} %key_weight.1, bf16[128,128]{1,0:T(8,128)(2,1)} %key_grad.1), custom_call_target="tpu_custom_call" | custom-call | flops 268435456 | bytes 4194304 | tf_op jit(solution)/shard_map/key_projection_backward/pallas_call | solution.py:297
  47.0 1.1 %write_results.1 = (bf16[128,1024]{1,0:T(8,128)(2,1)}, bf16[4,2,8,4,16,128]{5,4,3,2,1,0:T(8,128)(2,1)}, f32[1,128]{1,0:T(1,128)}) custom-call(bf16[128,1024]{1,0:T(8,128)(2,1)S(1)} %get-tuple-element.9.input_vmem, bf16[4,2,8,4,16,128]{5,4,3,2,1,0:T(8,128)(2,1)S(1)} %get-tuple-element.10.weight_vmem, f32[1,128]{1,0:T(1,128)S(1)} %get-tuple-element.11.bias_vmem), custom_call_target="tpu_custom_call" | custom-call | tf_op jit(solution)/shard_map/write_results/pallas_call | solution.py:325

commit v7 on v6

--- a/solution.py
+++ b/solution.py
@@ -119,7 +119,8 @@
     for copy in raw_copies[:-1]:
         copy.wait_recv()
 
-    first_columns = [pl.ds(pl.multiple_of(h * 2 * HD, 2 * HD), 2 * HD) for h in (pair, 1 - pair)]
+    farther = [(pair, 1 - pair), (1 - pair, pair)]
+    columns_of = [[pl.ds(pl.multiple_of(h * 2 * HD, 2 * HD), 2 * HD) for h in both] for both in farther]
 
     for j, g in enumerate(order):
         product = jnp.dot(
@@ -127,8 +128,8 @@
             preferred_element_type=jnp.float32,
         )
         parts[:, g] = product.astype(jnp.bfloat16).reshape(8, 16, HEADS * HD)
-        for h, columns in enumerate(first_columns if j == 0 else [pl.ds(0, HEADS * HD)]):
-            i = h if j == 0 else j + 1
+        for h, columns in enumerate(columns_of[j] if j < 2 else [pl.ds(0, HEADS * HD)]):
+            i = j * 2 + h if j < 2 else j + 2
             for kx in (2, 1, 3):
                 remote(parts.at[pl.ds(((x + kx) % 4) * 2, 2), g, :, columns], got.at[x, :, g, :, columns],
                        near_send.at[i], near_recv.at[i], near(kx, 0)).start()
@@ -139,9 +140,9 @@
 
     pl.semaphore_wait(two_away, 2)
     for j, g in enumerate(order):
-        if j == 0:
-            for i, (h, columns) in enumerate(zip((pair, 1 - pair), first_columns)):
-                wait_for(got.at[pl.ds(0, 3), :, g, :, columns], near_recv.at[i])
+        if j < 2:
+            for i, (h, columns) in enumerate(zip(farther[j], columns_of[j])):
+                wait_for(got.at[pl.ds(0, 3), :, g, :, columns], near_recv.at[j * 2 + i])
                 total = got[0, :, g, :, columns].astype(jnp.float32)
                 for s in range(1, 4):
                     total += got[s, :, g, :, columns].astype(jnp.float32)
@@ -150,7 +151,7 @@
                 for p in (1 - zp, zp):
                     remote(halves.at[there * 2 + p], got_far.at[z], far_send, far_recv, at(x, y, there, p, c)).start()
         else:
-            wait_for(got.at[pl.ds(0, 3), :, g], near_recv.at[j + 1])
+            wait_for(got.at[pl.ds(0, 3), :, g], near_recv.at[j + 2])
             total = got[0, :, g].astype(jnp.float32)
             for s in range(1, 4):
                 total += got[s, :, g].astype(jnp.float32)
@@ -228,10 +229,10 @@
 
     for copy in raw_copies + [normed_copy] + weight_copies:
         copy.wait_send()
-    for i in range(2):
-        wait_for(parts.at[pl.ds(0, 6), 0, :, first_columns[i]], near_send.at[i])
-    for j in range(1, GROUPS):
-        wait_for(parts.at[pl.ds(0, 6), 0], near_send.at[j + 1])
+    for i in range(4):
+        wait_for(parts.at[pl.ds(0, 6), 0, :, pl.ds(0, 2 * HD)], near_send.at[i])
+    for j in range(2, GROUPS):
+        wait_for(parts.at[pl.ds(0, 6), 0], near_send.at[j + 2])
     wait_for(halves.at[pl.ds(0, 15)], far_send)
     wait_for(bias_near.at[pl.ds(0, 3)], bias_send.at[0])
     wait_for(bias_far.at[pl.ds(0, 15)], bias_send.at[1])
@@ -314,7 +315,7 @@
             pltpu.VMEM((4, 1, HD), f32),
             pltpu.VMEM((16, 1, HD), f32),
             dma((3,)), dma((7,)), dma((7,)), dma, dma, dma((3,)), dma((3,)),
-            dma((5,)), dma((5,)), dma, dma, dma((16,)), dma((4,)), dma((4,)), dma((4,)),
+            dma((6,)), dma((6,)), dma, dma, dma((16,)), dma((4,)), dma((4,)), dma((4,)),
             dma((3,)), dma((3,)), dma, dma, dma,
             dma, dma, dma((2,)), dma((2,)), regular, regular,
         ],

time: 48.2 us -> 48 us (level)
  no operation moved by 1% of the time
where the time goes in v7:
time: 48 us; the launch traced here: 47.8 us
  Pallas kernels  47.2 us (98%)
  between operations  0.64 us (1%)
    pallas_call x1, Pallas kernels, body(): pl.pallas_call(kernel, out_shape=shapes, in_specs=[hbm] * 3, out_specs=(a...  46.1 us
    pallas_call x1, Pallas kernels, body(): pl.pallas_call(finish, out_shape=shapes, in_specs=[anywhere] * 3, out_spe...  1.08 us

profile of v7, /device:TPU:1, one launch (start us, length us, event | category | flops | bytes accessed | tf_op | source)
XLA Modules:
  0.0 47.8 jit_solution(4980753229384643855)
XLA Ops:
  0.6 46.1 %key_projection_backward.1 = (bf16[128,1024]{1,0:T(8,128)(2,1)S(1)}, bf16[4,2,8,4,16,128]{5,4,3,2,1,0:T(8,128)(2,1)S(1)}, f32[1,128]{1,0:T(1,128)S(1)}) custom-call(bf16[128,1024]{1,0:T(8,128)(2,1)} %normed.1, bf16[4096,128]{1,0:T(8,128)(2,1)} %key_weight.1, bf16[128,128]{1,0:T(8,128)(2,1)} %key_grad.1), custom_call_target="tpu_custom_call" | custom-call | flops 268435456 | bytes 4194304 | tf_op jit(solution)/shard_map/key_projection_backward/pallas_call | solution.py:298
  46.8 1.1 %write_results.1 = (bf16[128,1024]{1,0:T(8,128)(2,1)}, bf16[4,2,8,4,16,128]{5,4,3,2,1,0:T(8,128)(2,1)}, f32[1,128]{1,0:T(1,128)}) custom-call(bf16[128,1024]{1,0:T(8,128)(2,1)S(1)} %get-tuple-element.9.input_vmem, bf16[4,2,8,4,16,128]{5,4,3,2,1,0:T(8,128)(2,1)S(1)} %get-tuple-element.10.weight_vmem, f32[1,128]{1,0:T(1,128)S(1)} %get-tuple-element.11.bias_vmem), custom_call_target="tpu_custom_call" | custom-call | tf_op jit(solution)/shard_map/write_results/pallas_call | solution.py:326

commit v8 on v7

--- a/solution.py
+++ b/solution.py
@@ -163,7 +163,7 @@
                     continue
                 there = g * 2 + h
                 remote(halves.at[there * 2 + p], got_far.at[z], far_send, far_recv, at(x, y, there, p, c)).start()
-        if j == 0:
+        if j == GROUPS - 1:
             wait_for(bias_near.at[pl.ds(0, 3)], bias_recv.at[0])
             bias_far[z] = bias_near[0] + bias_near[1] + bias_near[2] + bias_near[3]
             for k in (8, 7, 9, 6, 10, 5, 11, 4, 12, 3, 13, 2, 14, 1, 15):

time: 48 us -> 47.8 us (level)
  no operation moved by 1% of the time
where the time goes in v8:
time: 47.8 us; the launch traced here: 47.6 us
  Pallas kernels  47 us (98%)
  between operations  0.64 us (1%)
    pallas_call x1, Pallas kernels, body(): pl.pallas_call(kernel, out_shape=shapes, in_specs=[hbm] * 3, out_specs=(a...  45.9 us
    pallas_call x1, Pallas kernels, body(): pl.pallas_call(finish, out_shape=shapes, in_specs=[anywhere] * 3, out_spe...  1.08 us

profile of v8, /device:TPU:1, one launch (start us, length us, event | category | flops | bytes accessed | tf_op | source)
XLA Modules:
  0.0 47.6 jit_solution(14739810325924861485)
XLA Ops:
  0.6 45.9 %key_projection_backward.1 = (bf16[128,1024]{1,0:T(8,128)(2,1)S(1)}, bf16[4,2,8,4,16,128]{5,4,3,2,1,0:T(8,128)(2,1)S(1)}, f32[1,128]{1,0:T(1,128)S(1)}) custom-call(bf16[128,1024]{1,0:T(8,128)(2,1)} %normed.1, bf16[4096,128]{1,0:T(8,128)(2,1)} %key_weight.1, bf16[128,128]{1,0:T(8,128)(2,1)} %key_grad.1), custom_call_target="tpu_custom_call" | custom-call | flops 268435456 | bytes 4194304 | tf_op jit(solution)/shard_map/key_projection_backward/pallas_call | solution.py:298
  46.6 1.1 %write_results.1 = (bf16[128,1024]{1,0:T(8,128)(2,1)}, bf16[4,2,8,4,16,128]{5,4,3,2,1,0:T(8,128)(2,1)}, f32[1,128]{1,0:T(1,128)}) custom-call(bf16[128,1024]{1,0:T(8,128)(2,1)S(1)} %get-tuple-element.9.input_vmem, bf16[4,2,8,4,16,128]{5,4,3,2,1,0:T(8,128)(2,1)S(1)} %get-tuple-element.10.weight_vmem, f32[1,128]{1,0:T(1,128)S(1)} %get-tuple-element.11.bias_vmem), custom_call_target="tpu_custom_call" | custom-call | tf_op jit(solution)/shard_map/write_results/pallas_call | solution.py:326

commit v9 on v8

--- a/solution.py
+++ b/solution.py
@@ -208,12 +208,6 @@
     for h in range(2):
         pl.when(pair * 2 + h == y)(own_tiles[h].start)
 
-    wait_for(bias_far.at[pl.ds(0, 15)], bias_recv.at[1])
-    bias_all = bias_far[0]
-    for s in range(1, 16):
-        bias_all += bias_far[s]
-    bias_grad[...] = bias_all * (1.0 / 128.0)
-
     load_weight.wait()
     for copy in weight_copies:
         copy.wait_recv()
@@ -249,6 +243,11 @@
             remote(block, block, wide_send.at[j], wide_recv.at[j], near(kx, kz)).start()
         if j == last:
             remote(block, block, cross_send, cross_recv, sibling).start()
+    wait_for(bias_far.at[pl.ds(0, 15)], bias_recv.at[1])
+    bias_all = bias_far[0]
+    for s in range(1, 16):
+        bias_all += bias_far[s]
+    bias_grad[...] = bias_all * (1.0 / 128.0)
     for copy, k, there in tile_copies:
         if k:
             copy.wait_send()

time: 47.8 us -> 47.8 us (level)
  no operation moved by 1% of the time
where the time goes in v9:
time: 47.8 us; the launch traced here: 47.6 us
  Pallas kernels  47 us (98%)
  between operations  0.64 us (1%)
    pallas_call x1, Pallas kernels, body(): pl.pallas_call(kernel, out_shape=shapes, in_specs=[hbm] * 3, out_specs=(a...  45.9 us
    pallas_call x1, Pallas kernels, body(): pl.pallas_call(finish, out_shape=shapes, in_specs=[anywhere] * 3, out_spe...  1.08 us

profile of v9, /device:TPU:1, one launch (start us, length us, event | category | flops | bytes accessed | tf_op | source)
XLA Modules:
  0.0 47.6 jit_solution(1100190205174535820)
XLA Ops:
  0.6 45.9 %key_projection_backward.1 = (bf16[128,1024]{1,0:T(8,128)(2,1)S(1)}, bf16[4,2,8,4,16,128]{5,4,3,2,1,0:T(8,128)(2,1)S(1)}, f32[1,128]{1,0:T(1,128)S(1)}) custom-call(bf16[128,1024]{1,0:T(8,128)(2,1)} %normed.1, bf16[4096,128]{1,0:T(8,128)(2,1)} %key_weight.1, bf16[128,128]{1,0:T(8,128)(2,1)} %key_grad.1), custom_call_target="tpu_custom_call" | custom-call | flops 268435456 | bytes 4194304 | tf_op jit(solution)/shard_map/key_projection_backward/pallas_call | solution.py:297
  46.6 1.1 %write_results.1 = (bf16[128,1024]{1,0:T(8,128)(2,1)}, bf16[4,2,8,4,16,128]{5,4,3,2,1,0:T(8,128)(2,1)}, f32[1,128]{1,0:T(1,128)}) custom-call(bf16[128,1024]{1,0:T(8,128)(2,1)S(1)} %get-tuple-element.9.input_vmem, bf16[4,2,8,4,16,128]{5,4,3,2,1,0:T(8,128)(2,1)S(1)} %get-tuple-element.10.weight_vmem, f32[1,128]{1,0:T(1,128)S(1)} %get-tuple-element.11.bias_vmem), custom_call_target="tpu_custom_call" | custom-call | tf_op jit(solution)/shard_map/write_results/pallas_call | solution.py:325
